TPU v7x, 512 devices: a whole 4x8x8 slice. The times are simulated.
512 devices in a mesh: dp: 16 (over y, x_lo), comp: 32 (over z, x_hi, core).
Axes of the slice: x: 4 (x_hi: 2, x_lo: 2; x = x_hi * 2 + x_lo), y: 8, z: 8, core: 2. Of those that a mesh axis runs over, the one named last changes fastest.
Arguments:
- descriptors: float32 [32768, 128], P(('dp', 'comp')), may hold values from -10 to 10
- means: float32 [128, 16384], P(None, 'comp'), may hold values from -0.8 to 0.8
- variances: float32 [128, 16384], P(None, 'comp'), may hold values from 0.25 to 2
- log_weights: float32 [16384], P('comp'), may hold values from -3 to 0
Outputs:
- new_means: float32 [128, 16384], P('dp', 'comp')
- new_variances: float32 [128, 16384], P('dp', 'comp')
- new_log_weights: float32 [16384], P('comp')
- mean_loglik: float32 [], replicated
All inputs are finite; a program needn't handle non-finite values.
Results may differ from a plain program's by a relative error of at most 0.0003.
Values sent between devices are 32-bit elements; how exact they have to be, the bound alone decides.
A program may use at most 64 MiB of HBM per device.

v0:
```python
import math
import jax
import jax.numpy as jnp
from jax import lax
from jax.sharding import PartitionSpec as P

LOG_TWO_PI = math.log(2.0 * math.pi)
PRIOR = 1.0


def matmul(left, right):
    return jnp.dot(left, right, precision=lax.Precision.HIGHEST, preferred_element_type=jnp.float32)


def local(descriptors, means, variances, log_weights):
    dims = means.shape[0]
    precision_mat = 1.0 / variances
    linear = means * precision_mat
    offset = (
        log_weights
        - 0.5 * jnp.sum(means * linear, 0)
        - 0.5 * jnp.sum(jnp.log(variances), 0)
        - 0.5 * dims * LOG_TWO_PI
    )
    local_rows = descriptors.shape[0]
    groups = lax.axis_size("comp")
    gathered_rows = local_rows * groups
    blocks = max(1, gathered_rows // 1024)
    block_size = gathered_rows // blocks
    comp_local = means.shape[1]
    gathered = lax.all_gather(descriptors, "comp", axis=0, tiled=True)
    counts = jnp.zeros((comp_local,), jnp.float32)
    first = jnp.zeros((dims, comp_local), jnp.float32)
    second = jnp.zeros((dims, comp_local), jnp.float32)
    loglik = jnp.zeros((), jnp.float32)
    for number in range(blocks):
        rows = gathered[number * block_size : (number + 1) * block_size]
        squares = rows * rows
        scores = -0.5 * matmul(squares, precision_mat) + matmul(rows, linear) + offset
        top = lax.pmax(jnp.max(scores, 1), "comp")
        total = lax.psum(jnp.sum(jnp.exp(scores - top[:, None]), 1), "comp")
        norm = top + jnp.log(total)
        resp = jnp.exp(scores - norm[:, None])
        counts = counts + jnp.sum(resp, 0)
        first = first + matmul(rows.T, resp)
        second = second + matmul(squares.T, resp)
        loglik = loglik + jnp.sum(norm)
    first_part, second_part = (
        lax.psum_scatter(first, "dp", scatter_dimension=0, tiled=True),
        lax.psum_scatter(second, "dp", scatter_dimension=0, tiled=True),
    )
    counts, loglik = lax.psum((counts, loglik), "dp")
    owned = first_part.shape[0]
    start = lax.axis_index("dp") * owned
    means_part = lax.dynamic_slice_in_dim(means, start, owned, 0)
    variances_part = lax.dynamic_slice_in_dim(variances, start, owned, 0)
    denom = counts + PRIOR
    new_means = (first_part + PRIOR * means_part) / denom
    scatter = second_part - 2.0 * means_part * first_part + means_part * means_part * counts
    new_variances = (scatter + PRIOR * variances_part) / denom
    total_rows = gathered_rows * lax.axis_size("dp")
    all_comps = comp_local * groups
    new_log_weights = jnp.log((counts + PRIOR) / (total_rows + all_comps * PRIOR))
    mean_loglik = loglik / (total_rows * dims)
    return (new_means, new_variances, new_log_weights, mean_loglik)


def solution(mesh):
    placed = (P(("dp", "comp"), None), P(None, "comp"), P(None, "comp"), P("comp"))
    return jax.shard_map(
        local,
        mesh=mesh,
        in_specs=placed,
        out_specs=(P("dp", "comp"), P("dp", "comp"), P("comp"), P()),
        check_vma=False,
    )
```

profile of v0, /device:TPU:4, one launch (start us, length us, event | category | flops | bytes accessed | tf_op | source)
XLA Modules:
  0.0 405.1 jit_solution(15663945424928719993)
XLA Ops:
  8.0 0.7 constant_dynamic-slice_fusion
  8.7 0.8 copy.23
  9.5 0.9 copy.24
  10.4 1.1 multiply_reduce_fusion
  12.2 85.8 %all-gather.2.cloned.1.call-done = f32[2048,128]{1,0:T(8,128)} async-done(((f32[64,128]{1,0:T(8,128)}), f32[2048,128]{1,0:T(8,128)}) %all-gather.2.cloned.1.call-update) | async-done | bytes 1048592 | tf_op jit(solution)/shard_map/all_gather | solution.py:31
  98.0 3.0 fusion.19
  101.1 1.8 fusion.16
  103.0 2.2 fusion.33
  105.1 3.5 fusion.34
  108.6 64.2 %all-reduce.1 = (f32[1024]{0:T(1024)S(1)}, f32[1024]{0:T(1024)S(1)}) all-reduce(f32[1024]{0:T(1024)S(1)} %get-tuple-element.28, f32[1024]{0:T(1024)S(1)} %get-tuple-element.30), channel_id=1, replica_groups=mesh['dp'=16,'comp'=32] {'comp'}, use_global_device_ids=true, to_apply=%region_3.0 | all-reduce | flops 2048 | bytes 16384 | tf_op jit(solution)/shard_map/pmax | solution.py:40
  172.9 1.9 exponential_reduce_fusion
  175.1 66.2 %all-reduce = (f32[1024]{0:T(1024)S(1)}, f32[1024]{0:T(1024)S(1)}) all-reduce(f32[1024]{0:T(1024)S(1)} %exponential_reduce_fusion.1, f32[1024]{0:T(1024)S(1)} %exponential_reduce_fusion), channel_id=1, replica_groups=mesh['dp'=16,'comp'=32] {'comp'}, use_global_device_ids=true, to_apply=%region_5.0 | all-reduce | flops 2048 | bytes 16384 | tf_op jit(solution)/shard_map/psum | solution.py:41
  241.9 1.9 fusion.4
  243.8 1.9 fusion.9
  245.7 0.9 copy.19
  246.6 2.5 fusion.2
  249.2 3.2 fusion.10
  252.4 2.0 fusion.6
  256.1 35.2 %all-reduce.2 = (f32[512]{0:T(512)S(1)}, f32[]{:T(128)}) all-reduce(f32[512]{0:T(512)S(1)} %add.82, f32[]{:T(128)S(6)} %add.87), channel_id=1, replica_groups=mesh['dp'=16,'comp'=32] {'dp'}, use_global_device_ids=true, to_apply=%region_13.0 | all-reduce | flops 513 | bytes 4104 | tf_op jit(solution)/shard_map/psum | solution.py:52
  292.5 28.4 %reduce-scatter.7.cloned.1.call-done = f32[8,512]{1,0:T(8,128)} async-done(((f32[128,512]{1,0:T(8,128)}), f32[8,512]{1,0:T(8,128)}) %reduce-scatter.7.cloned.1.call-update) | async-done | bytes 16400
  320.9 0.8 copy.20
  321.8 73.2 %reduce-scatter.9.cloned.1.call-done = f32[8,512]{1,0:T(8,128)} async-done(((f32[128,512]{1,0:T(8,128)}), f32[8,512]{1,0:T(8,128)}) %reduce-scatter.9.cloned.1.call-update) | async-done | bytes 16400
  395.0 0.8 copy.22
  396.1 0.7 copy.17
  (28 shorter events, 4.4 us)
Async XLA Ops:
  7.2 93.9 %copy-start.3 = (f32[128,512]{1,0:T(8,128)S(1)}, f32[128,512]{1,0:T(8,128)}, u32[]{:S(2)}) copy-start(f32[128,512]{1,0:T(8,128)} %param.6) | copy-start | bytes 786436
  7.2 90.8 %all-gather.2.cloned.1.call-start = ((), (), s32[]{:S(2)}) async-start(), calls=%async_computation.2 | async-start | bytes 1081344 | tf_op jit(solution)/shard_map/all_gather | solution.py:31
  7.9 313.0 %reduce-scatter.7.cloned.1.call-start = ((), (), s32[]{:S(2)}) async-start(), calls=%async_computation.3 | async-start | bytes 278528
  98.0 3.0 copy-start.2
  101.1 1.9 copy-start.4
  241.3 2.5 copy-start
  246.6 148.4 %reduce-scatter.9.cloned.1.call-start = ((), (), s32[]{:S(2)}) async-start(), calls=%async_computation.4 | async-start | bytes 278528
  246.6 2.5 copy-start.1
  252.4 143.4 %copy-start.5 = (f32[8,512]{0,1:T(8,128)S(1)}, f32[8,512]{0,1:T(8,128)}, u32[]{:S(2)}) copy-start(f32[8,512]{0,1:T(8,128)} %copy.23) | copy-start | bytes 49156
  252.4 143.4 %copy-start.6 = (f32[8,512]{0,1:T(8,128)S(1)}, f32[8,512]{0,1:T(8,128)}, u32[]{:S(2)}) copy-start(f32[8,512]{0,1:T(8,128)} %copy.24) | copy-start | bytes 49156
Sparse Core Ops, SparseCore 0:
  11.4 86.5 all-gather.1
  246.7 74.1 reduce-scatter.6
  324.0 70.9 reduce-scatter.8
where the time goes:
time: 406 us; the launch traced here: 405 us
  waiting for transfers between devices  188 us (46%)
  blocking collectives  166 us (41%)
  matrix products  20 us (5%)
  between operations  17 us (4%)
  other arithmetic  7.85 us (2%)
  local copies, waits for them, and re-layouts  6.41 us (2%)
    unnamed x5, waiting for transfers between devices  102 us
    all_gather x1, waiting for transfers between devices, local(): gathered = lax.all_gather(descriptors, 'comp', axis=0, tiled=True)  85.8 us
    psum x1, blocking collectives, local(): total = lax.psum(jnp.sum(jnp.exp(scores - top[:, None]), 1), 'comp')  66.2 us
    pmax x1, blocking collectives, local(): top = lax.pmax(jnp.max(scores, 1), 'comp')  64.2 us
    psum x1, blocking collectives, local(): counts, loglik = lax.psum((counts, loglik), 'dp')  35.2 us
    dot_general x8, matrix products, matmul(): jnp.dot(left, right, precision=lax.Precision.HIGHEST, preferred_element_t...  20 us
  transfers between devices with their start and end apart: 3, of which 3 were waited for; matrix products, arithmetic and copies ran while one was open for 3% of the time, Pallas kernels for 0%

commit v1 on v0

--- a/solution.py
+++ b/solution.py
@@ -28,7 +28,9 @@
     blocks = max(1, gathered_rows // 1024)
     block_size = gathered_rows // blocks
     comp_local = means.shape[1]
-    gathered = lax.all_gather(descriptors, "comp", axis=0, tiled=True)
+    gathered = jnp.concatenate(
+        lax.all_to_all(jnp.stack([descriptors] * lax.axis_size("comp")), "comp", 0, 0), axis=0
+    )
     counts = jnp.zeros((comp_local,), jnp.float32)
     first = jnp.zeros((dims, comp_local), jnp.float32)
     second = jnp.zeros((dims, comp_local), jnp.float32)

time: 406 us -> 356 us (0.88)
  waiting for transfers between devices: 188 us -> 130 us
  starting transfers between devices: 0.12 us -> 13.5 us
    all_gather x1 -> x0, waiting for transfers between devices: 85.8 us -> none  [local(): gathered = lax.all_gather(descriptors, 'comp', axis=0, tiled=True)]
    all_to_all x0 -> x1, waiting for transfers between devices: none -> 27 us  [local(): lax.all_to_all(jnp.stack([descriptors] * lax.axis_size('comp')), 'comp',...]
    all_to_all x0 -> x1, starting transfers between devices: none -> 13.4 us  [local(): lax.all_to_all(jnp.stack([descriptors] * lax.axis_size('comp')), 'comp',...]
    unnamed x5 -> x4, waiting for transfers between devices: 102 us -> 103 us
where the time goes in v1:
time: 356 us; the launch traced here: 355 us
  blocking collectives  162 us (46%)
  waiting for transfers between devices  130 us (37%)
  matrix products  18.8 us (5%)
  between operations  17.4 us (5%)
  starting transfers between devices  13.5 us (4%)
  local copies, waits for them, and re-layouts  7.67 us (2%)
  other arithmetic  6.14 us (2%)
    unnamed x4, waiting for transfers between devices  103 us
    psum x1, blocking collectives, local(): total = lax.psum(jnp.sum(jnp.exp(scores - top[:, None]), 1), 'comp')  66.2 us
    pmax x1, blocking collectives, local(): top = lax.pmax(jnp.max(scores, 1), 'comp')  60.5 us
    psum x1, blocking collectives, local(): counts, loglik = lax.psum((counts, loglik), 'dp')  35.3 us
    all_to_all x1, waiting for transfers between devices, local(): lax.all_to_all(jnp.stack([descriptors] * lax.axis_size('comp')), 'comp',...  27 us
    dot_general x8, matrix products, matmul(): jnp.dot(left, right, precision=lax.Precision.HIGHEST, preferred_element_t...  18.8 us
    all_to_all x1, starting transfers between devices, local(): lax.all_to_all(jnp.stack([descriptors] * lax.axis_size('comp')), 'comp',...  13.4 us
  transfers between devices with their start and end apart: 3, of which 3 were waited for; matrix products, arithmetic and copies ran while one was open for 3% of the time, Pallas kernels for 0%

profile of v1, /device:TPU:4, one launch (start us, length us, event | category | flops | bytes accessed | tf_op | source)
XLA Modules:
  0.0 355.3 jit_solution(14690133992147197365)
XLA Ops:
  7.2 1.9 stack.2
  9.1 13.4 %all-to-all-start = ((f32[32,64,128]{2,1,0:T(8,128)}), f32[32,64,128]{2,1,0:T(8,128)S(1)}, u32[]{:S(2)}, u32[]{:S(2)}) async-start(f32[32,64,128]{2,1,0:T(8,128)} %stack.2), calls=%async_computation | async-start | bytes 2097152 | tf_op jit(solution)/shard_map/all_to_all | solution.py:32
  22.7 0.8 copy.23
  23.5 0.9 copy.24
  24.5 27.0 %all-to-all-done = f32[32,64,128]{2,1,0:T(8,128)S(1)} async-done(((f32[32,64,128]{2,1,0:T(8,128)}), f32[32,64,128]{2,1,0:T(8,128)S(1)}, u32[]{:S(2)}, u32[]{:S(2)}) %all-to-all-start) | async-done | bytes 1048608 | tf_op jit(solution)/shard_map/all_to_all | solution.py:32
  51.6 1.8 fusion.16
  53.4 1.8 fusion.19
  55.3 3.5 fusion.27
  58.8 2.2 fusion.26
  61.0 60.5 %all-reduce.1 = (f32[1024]{0:T(1024)S(1)}, f32[1024]{0:T(1024)S(1)}) all-reduce(f32[1024]{0:T(1024)S(1)} %get-tuple-element.30, f32[1024]{0:T(1024)S(1)} %get-tuple-element.32), channel_id=1, replica_groups=mesh['dp'=16,'comp'=32] {'comp'}, use_global_device_ids=true, to_apply=%region_3.0 | all-reduce | flops 2048 | bytes 16384 | tf_op jit(solution)/shard_map/pmax | solution.py:42
  121.5 1.9 exponential_reduce_fusion
  123.8 66.2 %all-reduce = (f32[1024]{0:T(1024)S(1)}, f32[1024]{0:T(1024)S(1)}) all-reduce(f32[1024]{0:T(1024)S(1)} %exponential_reduce_fusion.1, f32[1024]{0:T(1024)S(1)} %exponential_reduce_fusion), channel_id=1, replica_groups=mesh['dp'=16,'comp'=32] {'comp'}, use_global_device_ids=true, to_apply=%region_5.0 | all-reduce | flops 2048 | bytes 16384 | tf_op jit(solution)/shard_map/psum | solution.py:43
  190.6 1.9 fusion.4
  192.5 1.9 fusion.9
  194.3 0.9 copy.19
  195.3 2.5 fusion.2
  197.8 3.2 fusion.10
  201.0 2.0 fusion.6
  204.7 35.3 %all-reduce.2 = (f32[512]{0:T(512)S(1)}, f32[]{:T(128)}) all-reduce(f32[512]{0:T(512)S(1)} %add.82, f32[]{:T(128)S(6)} %add.87), channel_id=1, replica_groups=mesh['dp'=16,'comp'=32] {'dp'}, use_global_device_ids=true, to_apply=%region_13.0 | all-reduce | flops 513 | bytes 4104 | tf_op jit(solution)/shard_map/psum | solution.py:54
  241.3 29.5 %reduce-scatter.7.cloned.1.call-done = f32[8,512]{1,0:T(8,128)} async-done(((f32[128,512]{1,0:T(8,128)}), f32[8,512]{1,0:T(8,128)}) %reduce-scatter.7.cloned.1.call-update) | async-done | bytes 16400
  270.8 0.8 copy.20
  271.6 73.2 %reduce-scatter.9.cloned.1.call-done = f32[8,512]{1,0:T(8,128)} async-done(((f32[128,512]{1,0:T(8,128)}), f32[8,512]{1,0:T(8,128)}) %reduce-scatter.9.cloned.1.call-update) | async-done | bytes 16400
  344.8 0.8 copy.22
  345.9 0.7 copy.17
  (31 shorter events, 3.2 us)
Async XLA Ops:
  7.2 15.5 %copy-start.2 = (f32[128,512]{1,0:T(8,128)S(1)}, f32[128,512]{1,0:T(8,128)}, u32[]{:S(2)}) copy-start(f32[128,512]{1,0:T(8,128)} %param.6) | copy-start | bytes 786436
  7.2 15.5 %copy-start.3 = (f32[128,512]{1,0:T(8,128)S(1)}, f32[128,512]{1,0:T(8,128)}, u32[]{:S(2)}) copy-start(f32[128,512]{1,0:T(8,128)} %param.5) | copy-start | bytes 786436
  7.2 17.3 %copy-start.7 = (f32[512]{0:T(512)S(1)}, f32[512]{0:T(512)}, u32[]{:S(2)}) copy-start(f32[512]{0:T(512)} %param.7) | copy-start | bytes 6148
  9.1 42.4 %all-to-all-start = ((f32[32,64,128]{2,1,0:T(8,128)}), f32[32,64,128]{2,1,0:T(8,128)S(1)}, u32[]{:S(2)}, u32[]{:S(2)}) async-start(f32[32,64,128]{2,1,0:T(8,128)} %stack.2), calls=%async_computation | async-start | bytes 2097152 | tf_op jit(solution)/shard_map/all_to_all | solution.py:32
  22.6 248.2 %reduce-scatter.7.cloned.1.call-start = ((), (), s32[]{:S(2)}) async-start(), calls=%async_computation.3 | async-start | bytes 278528
  53.4 1.9 copy-start.4
  190.0 2.5 copy-start
  195.2 149.6 %reduce-scatter.9.cloned.1.call-start = ((), (), s32[]{:S(2)}) async-start(), calls=%async_computation.4 | async-start | bytes 278528
  195.3 2.5 copy-start.1
  201.0 144.6 %copy-start.5 = (f32[8,512]{0,1:T(8,128)S(1)}, f32[8,512]{0,1:T(8,128)}, u32[]{:S(2)}) copy-start(f32[8,512]{0,1:T(8,128)} %copy.23) | copy-start | bytes 49156
  201.0 144.6 %copy-start.6 = (f32[8,512]{0,1:T(8,128)S(1)}, f32[8,512]{0,1:T(8,128)}, u32[]{:S(2)}) copy-start(f32[8,512]{0,1:T(8,128)} %copy.24) | copy-start | bytes 49156
Sparse Core Ops, SparseCore 0:
  195.3 75.3 reduce-scatter.6
  273.8 71.0 reduce-scatter.8
